TPU v7x, 32 devices: a whole 2x2x4 slice. The times are simulated.
32 devices in a mesh: team: 4 (over y, core), tm: 8 (over z, x).
Axes of the slice: x: 2, y: 2, z: 4, core: 2. Of those that a mesh axis runs over, the one named last changes fastest.
Arguments:
- transitions: float32 [4, 8, 512, 512], P('team', 'tm'), may hold values from -0.25 to 1.25
- states: float32 [4, 8, 64, 512], P('team', 'tm'), may hold values from -1 to 1
- cotangent: float32 [4, 8, 64, 512], P('team', 'tm'), may hold values from -2.4 to 2.4
- terminal: float32 [4, 64, 512], P('team'), may hold values from -6 to 6
- incidence: int32 [4, 8, 32, 2048], P('team', 'tm'), may hold values 0 or 1
- measured: float32 [4, 8, 64, 32], P('team', 'tm'), may hold values from -0.12 to 0.12
- obs_gain: float32 [4, 512], P('team'), may hold values from -6 to 6
Outputs:
- adjoint: float32 [4, 8, 64, 512], P('team', 'tm')
- grad_transitions: bfloat16 [4, 8, 512, 512], P('team', 'tm')
All inputs are finite; a program needn't handle non-finite values. No bound on the sum of `incidence` on one device may be relied on, other than what follows from the above.
Results may differ from a plain program's by a relative error of at most 0.001.
Values sent between devices are 32-bit elements; how exact they have to be, the bound alone decides.
A program may use at most 64 MiB of HBM per device.

v0:
```python
import jax
import jax.numpy as jnp
from jax import lax
from jax.sharding import PartitionSpec as P

STATES = 16
TEAM_STATES = 512
COLS = 64


HIGHEST = lax.Precision.HIGHEST


def from_behind(block, axis, distance):
    devices = range(lax.axis_size(axis))
    route = [(i - distance, i) for i in devices if i - distance in devices]
    return lax.ppermute(block, axis, route)


def matmul(left, right):
    return jnp.dot(left, right, precision=HIGHEST)


def shards(transitions, states, cotangent, terminal, incidence, measured, obs_gain):
    step_count = transitions.shape[1]
    matrices = transitions[0]
    incident = incidence[0].astype(jnp.float32)
    partial_value = jnp.einsum("scr,srl->scl", measured[0], incident, precision=HIGHEST)
    landmark = lax.psum(partial_value, "team")
    injection = jnp.einsum("scl,srl->scr", landmark, incident, precision=HIGHEST)
    driven = cotangent[0] + jnp.repeat(injection, STATES, axis=2) * obs_gain[0][None, None, :]
    offset = jnp.zeros((COLS, TEAM_STATES), jnp.float32)
    moment = 0
    offset = matmul(offset, matrices[moment]) + driven[moment]
    is_last = lax.axis_index("tm") == lax.axis_size("tm") - 1
    start_cot = jnp.where(is_last, terminal[0], jnp.zeros_like(terminal[0]))

    def advance_steps(turn, carried):
        outgoing = carried
        outgoing = matmul(outgoing, matrices[0])
        outgoing = outgoing + offset
        return from_behind(outgoing, "tm", -1) + start_cot

    incoming = lax.fori_loop(0, lax.axis_size("tm") - 1, advance_steps, start_cot)
    running = incoming
    adjoint_list = [None] * step_count
    grad_list = [None] * step_count
    moment = 0
    grad_now = jnp.einsum("cn,cm->nm", running, states[0, moment], precision=HIGHEST)
    grad_list[moment] = grad_now.astype(jnp.bfloat16)
    running = matmul(running, matrices[moment]) + driven[moment]
    adjoint_list[moment] = running
    adjoint = jnp.stack(adjoint_list)[None]
    grad_transitions = jnp.stack(grad_list)[None]
    return (adjoint, grad_transitions)


def solution(mesh):
    placed = (
        P("team", "tm", None, None),
        P("team", "tm", None, None),
        P("team", "tm", None, None),
        P("team", None, None),
        P("team", "tm", None, None),
        P("team", "tm", None, None),
        P("team", None),
    )
    return jax.shard_map(
        shards,
        mesh=mesh,
        in_specs=placed,
        out_specs=(P("team", "tm", None, None), P("team", "tm", None, None)),
        check_vma=False,
    )
```

profile of v0, /device:TPU:0, one launch (start us, length us, event | category | flops | bytes accessed | tf_op | source)
XLA Modules:
  0.0 120.3 jit_solution(8453081784988772054)
XLA Ops:
  7.2 0.0 copy-start
  7.2 0.0 all-reduce.2.cloned.1.call-start
  7.2 2.4 %fusion.7 = f32[64,2048]{1,0:T(8,128)} fusion(s32[1,1,32,2048]{3,2,1,0:T(8,128)} %param.13, f32[1,1,64,32]{2,3,1,0:T(8,128)} %param.14), kind=kOutput, calls=%fused_computation.11 | convolution fusion | flops 50397184 | bytes 794624 | tf_op jit(solution)/shard_map/scr,srl->scl/dot_general | solution.py:28
  9.6 0.0 copy-start.4
  9.6 0.0 copy-start.2
  9.6 0.0 all-reduce.2.cloned.1.call-update
  9.7 0.0 copy-start.1
  9.7 0.9 copy-done.4
  10.6 36.3 %all-reduce.2.cloned.1.call-done = f32[64,2048]{1,0:T(8,128)} async-done(((f32[64,2048]{1,0:T(8,128)}), f32[64,2048]{1,0:T(8,128)}) %all-reduce.2.cloned.1.call-update) | async-done | bytes 524304 | tf_op jit(solution)/shard_map/psum | solution.py:29
  46.9 0.0 copy-done.2
  46.9 1.6 %fusion.5 = f32[64,32]{0,1:T(8,128)S(1)} fusion(f32[64,2048]{1,0:T(8,128)} %all-reduce.2.cloned.1.call-done, s32[1,1,32,2048]{3,2,1,0:T(8,128)S(1)} %copy-done.2), kind=kOutput, calls=%fused_computation.9 | convolution fusion | flops 50397184 | bytes 794624 | tf_op jit(solution)/shard_map/scl,srl->scr/dot_general | solution.py:30
  48.5 0.0 copy-start.3
  48.5 0.0 copy-start.5
  48.5 0.1 copy.10
  48.6 0.0 copy-done.1
  48.6 0.8 copy-done.3
  49.4 0.0 copy-done.5
  49.4 0.8 convolution_add_fusion.2
  50.1 60.0 %while.10 = (s32[]{:T(128)}, f32[64,512]{1,0:T(8,128)S(1)}, f32[1,1,512,512]{3,2,1,0:T(8,128)S(1)}, f32[64,512]{1,0:T(8,128)S(1)}, f32[64,512]{1,0:T(8,128)S(1)}, /*index=5*/s32[]{:T(128)}) while((s32[]{:T(128)}, f32[64,512]{1,0:T(8,128)S(1)}, f32[1,1,512,512]{3,2,1,0:T(8,128)S(1)}, f32[64,512]{1,0:T(8,128)S(1)}, f32[64,512]{1,0:T(8,128)S(1)}, ...), condition=%wide.region_2.3_spmd, body=%wide.region_1.2_spmd.sunk | while | flops 201392128 | bytes 2359405 | solution.py:44
  50.2 0.8 convolution_add_fusion.4
  50.9 1.3 %collective-permute-start = (f32[64,512]{1,0:T(8,128)S(1)}, f32[64,512]{1,0:T(8,128)S(1)}, u32[]{:S(2)}, u32[]{:S(2)}) collective-permute-start(f32[64,512]{1,0:T(8,128)S(1)} %convolution_add_fusion.4), channel_id=1, source_target_pairs={{1,0},{2,1},{3,2},{4,3},{5,4},{6,5},{7,6},{9,8},{10,9},{11,10},{12... | collective-permute-start | bytes 393224 | tf_op jit(solution)/shard_map/while/body/eval_jaxpr/ppermute | solution.py:17
  52.2 5.6 %collective-permute-done = f32[64,512]{1,0:T(8,128)S(1)} collective-permute-done((f32[64,512]{1,0:T(8,128)S(1)}, f32[64,512]{1,0:T(8,128)S(1)}, u32[]{:S(2)}, u32[]{:S(2)}) %collective-permute-start) | collective-permute-done | bytes 131104 | tf_op jit(solution)/shard_map/while/body/eval_jaxpr/ppermute | solution.py:17
  57.8 0.8 convolution_add_fusion.4
  58.6 1.3 %collective-permute-start = (f32[64,512]{1,0:T(8,128)S(1)}, f32[64,512]{1,0:T(8,128)S(1)}, u32[]{:S(2)}, u32[]{:S(2)}) collective-permute-start(f32[64,512]{1,0:T(8,128)S(1)} %convolution_add_fusion.4), channel_id=1, source_target_pairs={{1,0},{2,1},{3,2},{4,3},{5,4},{6,5},{7,6},{9,8},{10,9},{11,10},{12... | collective-permute-start | bytes 393224 | tf_op jit(solution)/shard_map/while/body/eval_jaxpr/ppermute | solution.py:17
  59.9 5.9 %collective-permute-done = f32[64,512]{1,0:T(8,128)S(1)} collective-permute-done((f32[64,512]{1,0:T(8,128)S(1)}, f32[64,512]{1,0:T(8,128)S(1)}, u32[]{:S(2)}, u32[]{:S(2)}) %collective-permute-start) | collective-permute-done | bytes 131104 | tf_op jit(solution)/shard_map/while/body/eval_jaxpr/ppermute | solution.py:17
  65.8 0.8 convolution_add_fusion.4
  66.6 1.3 %collective-permute-start = (f32[64,512]{1,0:T(8,128)S(1)}, f32[64,512]{1,0:T(8,128)S(1)}, u32[]{:S(2)}, u32[]{:S(2)}) collective-permute-start(f32[64,512]{1,0:T(8,128)S(1)} %convolution_add_fusion.4), channel_id=1, source_target_pairs={{1,0},{2,1},{3,2},{4,3},{5,4},{6,5},{7,6},{9,8},{10,9},{11,10},{12... | collective-permute-start | bytes 393224 | tf_op jit(solution)/shard_map/while/body/eval_jaxpr/ppermute | solution.py:17
  67.9 6.5 %collective-permute-done = f32[64,512]{1,0:T(8,128)S(1)} collective-permute-done((f32[64,512]{1,0:T(8,128)S(1)}, f32[64,512]{1,0:T(8,128)S(1)}, u32[]{:S(2)}, u32[]{:S(2)}) %collective-permute-start) | collective-permute-done | bytes 131104 | tf_op jit(solution)/shard_map/while/body/eval_jaxpr/ppermute | solution.py:17
  74.4 0.8 convolution_add_fusion.4
  75.1 1.3 %collective-permute-start = (f32[64,512]{1,0:T(8,128)S(1)}, f32[64,512]{1,0:T(8,128)S(1)}, u32[]{:S(2)}, u32[]{:S(2)}) collective-permute-start(f32[64,512]{1,0:T(8,128)S(1)} %convolution_add_fusion.4), channel_id=1, source_target_pairs={{1,0},{2,1},{3,2},{4,3},{5,4},{6,5},{7,6},{9,8},{10,9},{11,10},{12... | collective-permute-start | bytes 393224 | tf_op jit(solution)/shard_map/while/body/eval_jaxpr/ppermute | solution.py:17
  76.4 6.5 %collective-permute-done = f32[64,512]{1,0:T(8,128)S(1)} collective-permute-done((f32[64,512]{1,0:T(8,128)S(1)}, f32[64,512]{1,0:T(8,128)S(1)}, u32[]{:S(2)}, u32[]{:S(2)}) %collective-permute-start) | collective-permute-done | bytes 131104 | tf_op jit(solution)/shard_map/while/body/eval_jaxpr/ppermute | solution.py:17
  82.9 0.8 convolution_add_fusion.4
  83.7 1.3 %collective-permute-start = (f32[64,512]{1,0:T(8,128)S(1)}, f32[64,512]{1,0:T(8,128)S(1)}, u32[]{:S(2)}, u32[]{:S(2)}) collective-permute-start(f32[64,512]{1,0:T(8,128)S(1)} %convolution_add_fusion.4), channel_id=1, source_target_pairs={{1,0},{2,1},{3,2},{4,3},{5,4},{6,5},{7,6},{9,8},{10,9},{11,10},{12... | collective-permute-start | bytes 393224 | tf_op jit(solution)/shard_map/while/body/eval_jaxpr/ppermute | solution.py:17
  85.0 6.9 %collective-permute-done = f32[64,512]{1,0:T(8,128)S(1)} collective-permute-done((f32[64,512]{1,0:T(8,128)S(1)}, f32[64,512]{1,0:T(8,128)S(1)}, u32[]{:S(2)}, u32[]{:S(2)}) %collective-permute-start) | collective-permute-done | bytes 131104 | tf_op jit(solution)/shard_map/while/body/eval_jaxpr/ppermute | solution.py:17
  91.8 0.8 convolution_add_fusion.4
  92.6 1.3 %collective-permute-start = (f32[64,512]{1,0:T(8,128)S(1)}, f32[64,512]{1,0:T(8,128)S(1)}, u32[]{:S(2)}, u32[]{:S(2)}) collective-permute-start(f32[64,512]{1,0:T(8,128)S(1)} %convolution_add_fusion.4), channel_id=1, source_target_pairs={{1,0},{2,1},{3,2},{4,3},{5,4},{6,5},{7,6},{9,8},{10,9},{11,10},{12... | collective-permute-start | bytes 393224 | tf_op jit(solution)/shard_map/while/body/eval_jaxpr/ppermute | solution.py:17
  93.9 8.0 %collective-permute-done = f32[64,512]{1,0:T(8,128)S(1)} collective-permute-done((f32[64,512]{1,0:T(8,128)S(1)}, f32[64,512]{1,0:T(8,128)S(1)}, u32[]{:S(2)}, u32[]{:S(2)}) %collective-permute-start) | collective-permute-done | bytes 131104 | tf_op jit(solution)/shard_map/while/body/eval_jaxpr/ppermute | solution.py:17
  101.9 0.8 convolution_add_fusion.4
  102.7 1.3 %collective-permute-start = (f32[64,512]{1,0:T(8,128)S(1)}, f32[64,512]{1,0:T(8,128)S(1)}, u32[]{:S(2)}, u32[]{:S(2)}) collective-permute-start(f32[64,512]{1,0:T(8,128)S(1)} %convolution_add_fusion.4), channel_id=1, source_target_pairs={{1,0},{2,1},{3,2},{4,3},{5,4},{6,5},{7,6},{9,8},{10,9},{11,10},{12... | collective-permute-start | bytes 393224 | tf_op jit(solution)/shard_map/while/body/eval_jaxpr/ppermute | solution.py:17
  104.0 6.2 %collective-permute-done = f32[64,512]{1,0:T(8,128)S(1)} collective-permute-done((f32[64,512]{1,0:T(8,128)S(1)}, f32[64,512]{1,0:T(8,128)S(1)}, u32[]{:S(2)}, u32[]{:S(2)}) %collective-permute-start) | collective-permute-done | bytes 131104 | tf_op jit(solution)/shard_map/while/body/eval_jaxpr/ppermute | solution.py:17
  110.2 1.4 %fusion.2 = f32[1,1,64,512]{3,2,1,0:T(8,128)} fusion(f32[64,512]{1,0:T(8,128)S(1)} %get-tuple-element.29, f32[1,1,512,512]{3,2,1,0:T(8,128)S(1)} %get-tuple-element.90, f32[64,512]{1,0:T(8,128)S(1)} %copy.10, f32[512]{0:T(512)S(1)} %bitcast.43, f32[1,1,64,512]{3,2,1,0:T(8,128)S(1)} %copy-done.3), kind=kOutput, calls=%fused_computation.5 | convolution fusion | flops 201424896 | bytes 1574912 | tf_op jit(solution)/shard_map/dot_general | solution.py:21
  111.6 0.0 copy-done
  111.6 1.8 %fusion.1 = bf16[1,1,512,512]{3,2,1,0:T(8,128)(2,1)} fusion(f32[64,512]{1,0:T(8,128)S(1)} %get-tuple-element.29, f32[1,1,64,512]{3,2,1,0:T(8,128)S(1)} %copy-done), kind=kOutput, calls=%fused_computation.3 | convolution fusion | flops 201588736 | bytes 786432 | tf_op jit(solution)/shard_map/cn,cm->nm/dot_general | solution.py:49
  (10 shorter events, 0.2 us)
Async XLA Ops:
  7.2 104.5 %copy-start = (f32[1,1,64,512]{3,2,1,0:T(8,128)S(1)}, f32[1,1,64,512]{3,2,1,0:T(8,128)}, u32[]{:S(2)}) copy-start(f32[1,1,64,512]{3,2,1,0:T(8,128)} %param.10) | copy-start | bytes 393220
  7.2 39.7 %all-reduce.2.cloned.1.call-start = ((), (), s32[]{:S(2)}) async-start(), calls=%async_computation | async-start | bytes 1048576 | tf_op jit(solution)/shard_map/psum | solution.py:29
  9.6 0.9 copy-start.4
  9.6 37.2 %copy-start.2 = (s32[1,1,32,2048]{3,2,1,0:T(8,128)S(1)}, s32[1,1,32,2048]{3,2,1,0:T(8,128)}, u32[]{:S(2)}) copy-start(s32[1,1,32,2048]{3,2,1,0:T(8,128)} %param.13) | copy-start | bytes 786436
  9.7 39.0 %copy-start.1 = (f32[1,1,512,512]{3,2,1,0:T(8,128)S(1)}, f32[1,1,512,512]{3,2,1,0:T(8,128)}, u32[]{:S(2)}) copy-start(f32[1,1,512,512]{3,2,1,0:T(8,128)} %param.9) | copy-start | bytes 3145732
  48.5 0.9 copy-start.3
  48.5 0.9 copy-start.5
  50.9 6.9 %collective-permute-start = (f32[64,512]{1,0:T(8,128)S(1)}, f32[64,512]{1,0:T(8,128)S(1)}, u32[]{:S(2)}, u32[]{:S(2)}) collective-permute-start(f32[64,512]{1,0:T(8,128)S(1)} %convolution_add_fusion.4), channel_id=1, source_target_pairs={{1,0},{2,1},{3,2},{4,3},{5,4},{6,5},{7,6},{9,8},{10,9},{11,10},{12... | collective-permute-start | bytes 393224 | tf_op jit(solution)/shard_map/while/body/eval_jaxpr/ppermute | solution.py:17
  58.6 7.2 %collective-permute-start = (f32[64,512]{1,0:T(8,128)S(1)}, f32[64,512]{1,0:T(8,128)S(1)}, u32[]{:S(2)}, u32[]{:S(2)}) collective-permute-start(f32[64,512]{1,0:T(8,128)S(1)} %convolution_add_fusion.4), channel_id=1, source_target_pairs={{1,0},{2,1},{3,2},{4,3},{5,4},{6,5},{7,6},{9,8},{10,9},{11,10},{12... | collective-permute-start | bytes 393224 | tf_op jit(solution)/shard_map/while/body/eval_jaxpr/ppermute | solution.py:17
  66.6 7.8 %collective-permute-start = (f32[64,512]{1,0:T(8,128)S(1)}, f32[64,512]{1,0:T(8,128)S(1)}, u32[]{:S(2)}, u32[]{:S(2)}) collective-permute-start(f32[64,512]{1,0:T(8,128)S(1)} %convolution_add_fusion.4), channel_id=1, source_target_pairs={{1,0},{2,1},{3,2},{4,3},{5,4},{6,5},{7,6},{9,8},{10,9},{11,10},{12... | collective-permute-start | bytes 393224 | tf_op jit(solution)/shard_map/while/body/eval_jaxpr/ppermute | solution.py:17
  75.1 7.8 %collective-permute-start = (f32[64,512]{1,0:T(8,128)S(1)}, f32[64,512]{1,0:T(8,128)S(1)}, u32[]{:S(2)}, u32[]{:S(2)}) collective-permute-start(f32[64,512]{1,0:T(8,128)S(1)} %convolution_add_fusion.4), channel_id=1, source_target_pairs={{1,0},{2,1},{3,2},{4,3},{5,4},{6,5},{7,6},{9,8},{10,9},{11,10},{12... | collective-permute-start | bytes 393224 | tf_op jit(solution)/shard_map/while/body/eval_jaxpr/ppermute | solution.py:17
  83.7 8.1 %collective-permute-start = (f32[64,512]{1,0:T(8,128)S(1)}, f32[64,512]{1,0:T(8,128)S(1)}, u32[]{:S(2)}, u32[]{:S(2)}) collective-permute-start(f32[64,512]{1,0:T(8,128)S(1)} %convolution_add_fusion.4), channel_id=1, source_target_pairs={{1,0},{2,1},{3,2},{4,3},{5,4},{6,5},{7,6},{9,8},{10,9},{11,10},{12... | collective-permute-start | bytes 393224 | tf_op jit(solution)/shard_map/while/body/eval_jaxpr/ppermute | solution.py:17
  92.6 9.3 %collective-permute-start = (f32[64,512]{1,0:T(8,128)S(1)}, f32[64,512]{1,0:T(8,128)S(1)}, u32[]{:S(2)}, u32[]{:S(2)}) collective-permute-start(f32[64,512]{1,0:T(8,128)S(1)} %convolution_add_fusion.4), channel_id=1, source_target_pairs={{1,0},{2,1},{3,2},{4,3},{5,4},{6,5},{7,6},{9,8},{10,9},{11,10},{12... | collective-permute-start | bytes 393224 | tf_op jit(solution)/shard_map/while/body/eval_jaxpr/ppermute | solution.py:17
  102.7 7.5 %collective-permute-start = (f32[64,512]{1,0:T(8,128)S(1)}, f32[64,512]{1,0:T(8,128)S(1)}, u32[]{:S(2)}, u32[]{:S(2)}) collective-permute-start(f32[64,512]{1,0:T(8,128)S(1)} %convolution_add_fusion.4), channel_id=1, source_target_pairs={{1,0},{2,1},{3,2},{4,3},{5,4},{6,5},{7,6},{9,8},{10,9},{11,10},{12... | collective-permute-start | bytes 393224 | tf_op jit(solution)/shard_map/while/body/eval_jaxpr/ppermute | solution.py:17
Sparse Core Ops, SparseCore 0:
  10.9 35.8 all-reduce.1
where the time goes:
time: 121 us; the launch traced here: 120 us
  waiting for transfers between devices  81.7 us (68%)
  between operations  14.1 us (12%)
  matrix products  13.3 us (11%)
  starting transfers between devices  9.05 us (7%)
  local copies, waits for them, and re-layouts  1.78 us (1%)
    ppermute x7, waiting for transfers between devices, from_behind(): return lax.ppermute(block, axis, route)  45.4 us
    psum x1, waiting for transfers between devices, shards(): landmark = lax.psum(partial_value, 'team')  36.3 us
    ppermute x7, starting transfers between devices, from_behind(): return lax.ppermute(block, axis, route)  9.01 us
    dot_general x9, matrix products, matmul(): return jnp.dot(left, right, precision=HIGHEST)  7.44 us
  transfers between devices with their start and end apart: 8, of which 8 were waited for; matrix products, arithmetic and copies ran while one was open for 0% of the time, Pallas kernels for 0%

commit v1 on v0

v1 whole, which is shorter than its diff:
```python
import functools

import jax
import jax.numpy as jnp
from jax import lax
from jax.experimental import pallas as pl
from jax.experimental.pallas import tpu as pltpu
from jax.sharding import PartitionSpec as P

CHUNKS = 4
F32 = jnp.float32
BF16 = jnp.bfloat16
MESH = pl.DeviceIdType.MESH


def split(value):
    high = value.astype(BF16)
    return high, (value - high.astype(F32)).astype(BF16)


def dot(left, right, dims=((1,), (0,))):
    return lax.dot_general(left, right, (dims, ((), ())), preferred_element_type=F32)


def kernel(
    teams, steps, chunks,
    t_hbm, s_hbm, cot_hbm, term_hbm, inc_hbm, meas_hbm, gain_hbm,
    adj_hbm, grad_hbm,
    t_vm, s_vm, gain_vm, th, tl, s3, x3, xin, drv, out, grad,
    meas, inc, part, parts,
    local_sem, inc_send, inc_recv, meas_send, meas_recv, part_send, part_recv,
    x_send, x_recv, out_sem, grad_sem,
):
    me = lax.axis_index("team")
    step = lax.axis_index("tm")
    last = step == steps - 1
    first = step == 0
    cols, width = xin.shape
    robots, cut = inc.shape[1:]
    rows = cols // chunks
    peers = [lax.rem(me + d, teams) for d in range(teams)]
    behind = [lax.rem(me + teams - d, teams) for d in range(teams)]

    barrier = pltpu.get_barrier_semaphore()
    for d in range(1, teams):
        pl.semaphore_signal(barrier, inc=1, device_id={"team": peers[d]}, device_id_type=MESH)

    @pl.when(step > 0)
    def _():
        pl.semaphore_signal(barrier, inc=1, device_id={"tm": step - 1}, device_id_type=MESH)

    @pl.when(step < steps - 1)
    def _():
        pl.semaphore_signal(barrier, inc=1, device_id={"tm": step + 1}, device_id_type=MESH)

    def columns(owner):
        return inc_hbm.at[0, 0, :, pl.ds(pl.multiple_of(owner * cut, cut), cut)]

    loads = [
        pltpu.make_async_copy(t_hbm.at[0, 0], t_vm, local_sem.at[0]),
        pltpu.make_async_copy(cot_hbm.at[0, 0], drv, local_sem.at[1]),
        pltpu.make_async_copy(s_hbm.at[0, 0], s_vm, local_sem.at[2]),
        pltpu.make_async_copy(meas_hbm.at[0, 0], meas.at[0], local_sem.at[3]),
        pltpu.make_async_copy(gain_hbm, gain_vm, local_sem.at[4]),
        pltpu.make_async_copy(columns(me), inc.at[0], local_sem.at[5]),
    ]
    for load in loads:
        load.start()
    terminal = pltpu.make_async_copy(term_hbm.at[0], xin, local_sem.at[6])

    @pl.when(last)
    def _():
        terminal.start()

    inc_copies = [None] + [
        pltpu.make_async_remote_copy(
            src_ref=columns(peers[d]), dst_ref=inc.at[d],
            send_sem=inc_send.at[d], recv_sem=inc_recv.at[d],
            device_id={"team": peers[d]}, device_id_type=MESH)
        for d in range(1, teams)
    ]
    meas_copies = [None] + [
        pltpu.make_async_remote_copy(
            src_ref=meas_hbm.at[0, 0], dst_ref=meas.at[d],
            send_sem=meas_send.at[d], recv_sem=meas_recv.at[d],
            device_id={"team": peers[d]}, device_id_type=MESH)
        for d in range(1, teams)
    ]
    neighbours = (step > 0).astype(jnp.int32) + (step < steps - 1).astype(jnp.int32)
    pl.semaphore_wait(barrier, teams - 1 + neighbours)
    for d in range(1, teams):
        meas_copies[d].start()
        inc_copies[d].start()

    loads[0].wait()

    @pl.loop(0, width // 64)
    def _(i):
        band = pl.ds(pl.multiple_of(i * 64, 64), 64)
        high, low = split(t_vm[band, :])
        th[band, :] = high
        tl[band, :] = low

    loads[1].wait()
    loads[2].wait()
    high, low = split(s_vm[...])
    s3[0:cols, :] = high
    s3[cols:2 * cols, :] = high
    s3[2 * cols:3 * cols, :] = low

    def times_transition(high, low):
        both = jnp.concatenate([high, low], axis=0)
        wide = dot(both, th[...])
        n = high.shape[0]
        return wide[:n] + wide[n:] + dot(high, tl[...])

    def keep(at, n, high, low):
        x3[at:at + n, :] = high
        x3[cols + at:cols + at + n, :] = low
        x3[2 * cols + at:2 * cols + at + n, :] = high

    @pl.when(last)
    def _():
        terminal.wait()
        high, low = split(xin[...])
        keep(0, cols, high, low)
        drv[...] += times_transition(high, low)

    loads[3].wait()
    loads[4].wait()
    loads[5].wait()
    landmark = jnp.zeros((2 * cols, cut), F32)
    seen = []
    for d in range(teams):
        if d:
            meas_copies[d].wait_recv()
            inc_copies[d].wait_recv()
        seen.append(inc[d].astype(F32).astype(BF16))
        high, low = split(meas[d])
        landmark = landmark + dot(jnp.concatenate([high, low], axis=0), seen[d])
    high, low = split(landmark[:cols] + landmark[cols:])
    both = jnp.concatenate([high, low], axis=0)
    part_copies = [None]
    for d in range(teams):
        piece = dot(both, seen[d], ((1,), (1,)))
        piece = piece[:cols] + piece[cols:]
        if d == 0:
            parts[0] = piece
            continue
        part[d] = piece
        copy = pltpu.make_async_remote_copy(
            src_ref=part.at[d], dst_ref=parts.at[d],
            send_sem=part_send.at[d], recv_sem=part_recv.at[d],
            device_id={"team": behind[d]}, device_id_type=MESH)
        copy.start()
        part_copies.append(copy)

    states = width // robots
    robot = lax.broadcasted_iota(jnp.int32, (robots, width), 0)
    state = lax.broadcasted_iota(jnp.int32, (robots, width), 1)
    lower = robot * states
    pick = jnp.where((state >= lower) & (state < lower + states), 1.0, 0.0).astype(BF16)
    injection = parts[0]
    for d in range(1, teams):
        part_copies[d].wait_recv()
        injection = injection + parts[d]
    high, low = split(injection)
    spread = dot(jnp.concatenate([high, low], axis=0), pick)
    drv[...] += (spread[:cols] + spread[cols:]) * gain_vm[...]

    x_copies = [
        pltpu.make_async_remote_copy(
            src_ref=out.at[pl.ds(i * rows, rows)], dst_ref=xin.at[pl.ds(i * rows, rows)],
            send_sem=x_send.at[i], recv_sem=x_recv.at[i],
            device_id={"tm": lax.max(step - 1, 0)}, device_id_type=MESH)
        for i in range(chunks)
    ]
    out_copies = [
        pltpu.make_async_copy(
            out.at[pl.ds(i * rows, rows)], adj_hbm.at[0, 0, pl.ds(i * rows, rows)], out_sem.at[i])
        for i in range(chunks)
    ]
    for i in range(chunks):
        at = i * rows

        @pl.when(last)
        def _():
            out[at:at + rows, :] = drv[at:at + rows, :]

        @pl.when(step < steps - 1)
        def _():
            x_copies[i].wait_recv()
            high, low = split(xin[at:at + rows, :])
            out[at:at + rows, :] = times_transition(high, low) + drv[at:at + rows, :]
            keep(at, rows, high, low)

        @pl.when(step > 0)
        def _():
            x_copies[i].start()

        out_copies[i].start()

    blocks = grad_sem.shape[0]
    high = width // blocks
    grad_copies = []
    for b in range(blocks):
        band = slice(b * high, (b + 1) * high)
        grad[band, :] = dot(x3[:, band], s3[...], ((0,), (0,))).astype(BF16)
        copy = pltpu.make_async_copy(
            grad.at[pl.ds(b * high, high)], grad_hbm.at[0, 0, pl.ds(b * high, high)], grad_sem.at[b])
        copy.start()
        grad_copies.append(copy)

    for d in range(1, teams):
        inc_copies[d].wait_send()
        meas_copies[d].wait_send()
        part_copies[d].wait_send()

    @pl.when(step > 0)
    def _():
        for copy in x_copies:
            copy.wait_send()

    for copy in out_copies + grad_copies:
        copy.wait()


def shards(teams, steps, transitions, states, cotangent, terminal, incidence, measured, obs_gain):
    cols, width = terminal.shape[1:]
    robots, landmarks = incidence.shape[2:]
    cut = landmarks // teams
    chunks = CHUNKS
    blocks = 4
    dma = pltpu.SemaphoreType.DMA
    anywhere = pl.BlockSpec(memory_space=pl.ANY)
    return pl.pallas_call(
        functools.partial(kernel, teams, steps, chunks),
        out_shape=(
            jax.ShapeDtypeStruct((1, 1, cols, width), F32),
            jax.ShapeDtypeStruct((1, 1, width, width), BF16),
        ),
        in_specs=[anywhere] * 7,
        out_specs=(anywhere, anywhere),
        scratch_shapes=[
            pltpu.VMEM((width, width), F32),
            pltpu.VMEM((cols, width), F32),
            pltpu.VMEM((1, width), F32),
            pltpu.VMEM((width, width), BF16),
            pltpu.VMEM((width, width), BF16),
            pltpu.VMEM((3 * cols, width), BF16),
            pltpu.VMEM((3 * cols, width), BF16),
            pltpu.VMEM((cols, width), F32),
            pltpu.VMEM((cols, width), F32),
            pltpu.VMEM((cols, width), F32),
            pltpu.VMEM((width, width), BF16),
            pltpu.VMEM((teams, cols, robots), F32),
            pltpu.VMEM((teams, robots, cut), jnp.int32),
            pltpu.VMEM((teams, cols, robots), F32),
            pltpu.VMEM((teams, cols, robots), F32),
            dma((7,)),
            dma((teams,)), dma((teams,)), dma((teams,)), dma((teams,)), dma((teams,)), dma((teams,)),
            dma((chunks,)), dma((chunks,)), dma((chunks,)), dma((blocks,)),
        ],
        compiler_params=pltpu.CompilerParams(
            collective_id=0, has_side_effects=True, vmem_limit_bytes=32 * 1024 * 1024),
    )(transitions, states, cotangent, terminal, incidence, measured, obs_gain)


def solution(mesh):
    placed = (
        P("team", "tm", None, None),
        P("team", "tm", None, None),
        P("team", "tm", None, None),
        P("team", None, None),
        P("team", "tm", None, None),
        P("team", "tm", None, None),
        P("team", None),
    )
    return jax.shard_map(
        functools.partial(shards, mesh.shape["team"], mesh.shape["tm"]),
        mesh=mesh,
        in_specs=placed,
        out_specs=(P("team", "tm", None, None), P("team", "tm", None, None)),
        check_vma=False,
    )
```

time: 121 us -> 49.2 us (0.41)
  waiting for transfers between devices: 81.7 us -> 0 us
  Pallas kernels: 0 us -> 41.2 us
  between operations: 14.1 us -> 0.66 us
  matrix products: 13.3 us -> 0 us
  starting transfers between devices: 9.05 us -> 0 us
  local copies, waits for them, and re-layouts: 1.78 us -> 7.14 us
    ppermute x7 -> x0, waiting for transfers between devices: 45.4 us -> none  [from_behind(): return lax.ppermute(block, axis, route)]
    pallas_call x0 -> x1, Pallas kernels: none -> 41.2 us  [shards(): pl.pallas_call(functools.partial(kernel, teams, steps, chunks), out_shape...]
    psum x1 -> x0, waiting for transfers between devices: 36.3 us -> none  [shards(): landmark = lax.psum(partial_value, 'team')]
    dot_general x12 -> x0, matrix products: 13.3 us -> none  [the longest x9 7.44 us: matmul(): return jnp.dot(left, right, precision=HIGHEST)]
    ppermute x7 -> x0, starting transfers between devices: 9.01 us -> none  [from_behind(): return lax.ppermute(block, axis, route)]
    unnamed x13 -> x15, local copies, waits for them, and re-layouts: 1.65 us -> 7.14 us
  transfers between devices with their start and end apart: 8 -> 0, of which waited for: 8 -> 0; matrix products, arithmetic and copies ran while one was open for 0% -> 0% of each run, Pallas kernels for 0% -> 0%
where the time goes in v1:
time: 49.2 us; the launch traced here: 49 us
  Pallas kernels  41.2 us (84%)
  local copies, waits for them, and re-layouts  7.14 us (15%)
  between operations  0.66 us (1%)
    pallas_call x1, Pallas kernels, shards(): pl.pallas_call(functools.partial(kernel, teams, steps, chunks), out_shape...  41.2 us
    unnamed x15, local copies, waits for them, and re-layouts  7.14 us

profile of v1, /device:TPU:0, one launch (start us, length us, event | category | flops | bytes accessed | tf_op | source)
XLA Modules:
  0.0 49.0 jit_solution(15922757199680163084)
XLA Ops:
  0.6 0.0 copy-start.5
  0.6 0.8 %copy.9.meas_hbm = f32[1,1,64,32]{3,2,1,0:T(8,128)S(1)} copy(f32[1,1,64,32]{2,3,1,0:T(8,128)} %param.12) | data formatting | bytes 16384 | tf_op args[5]
  1.4 0.0 copy-done.5
  1.4 0.0 copy-start
  1.5 1.2 %copy-done = f32[1,1,512,512]{3,2,1,0:T(8,128)S(1)} copy-done((f32[1,1,512,512]{3,2,1,0:T(8,128)S(1)}, f32[1,1,512,512]{3,2,1,0:T(8,128)}, u32[]{:S(2)}) %copy-start) | copy-done | bytes 1048600
  2.7 0.0 copy-start.1
  2.7 0.9 %copy-done.1 = s32[1,1,32,2048]{3,2,1,0:T(8,128)S(1)} copy-done((s32[1,1,32,2048]{3,2,1,0:T(8,128)S(1)}, s32[1,1,32,2048]{3,2,1,0:T(8,128)}, u32[]{:S(2)}) %copy-start.1) | copy-done | bytes 262168
  3.6 0.0 copy-start.2
  3.6 0.9 %copy-done.2 = f32[1,1,64,512]{3,2,1,0:T(8,128)S(1)} copy-done((f32[1,1,64,512]{3,2,1,0:T(8,128)S(1)}, f32[1,1,64,512]{3,2,1,0:T(8,128)}, u32[]{:S(2)}) %copy-start.2) | copy-done | bytes 131096
  4.5 0.0 copy-start.3
  4.5 0.9 %copy-done.3 = f32[1,1,64,512]{3,2,1,0:T(8,128)S(1)} copy-done((f32[1,1,64,512]{3,2,1,0:T(8,128)S(1)}, f32[1,1,64,512]{3,2,1,0:T(8,128)}, u32[]{:S(2)}) %copy-start.3) | copy-done | bytes 131096
  5.4 0.0 copy-start.4
  5.4 0.9 %copy-done.4 = f32[1,64,512]{2,1,0:T(8,128)S(1)} copy-done((f32[1,64,512]{2,1,0:T(8,128)S(1)}, f32[1,64,512]{2,1,0:T(8,128)}, u32[]{:S(2)}) %copy-start.4) | copy-done | bytes 131096
  6.3 41.2 %shard_map.86 = (f32[1,1,64,512]{3,2,1,0:T(8,128)S(1)}, bf16[1,1,512,512]{3,2,1,0:T(8,128)(2,1)S(1)}) custom-call(f32[1,1,512,512]{3,2,1,0:T(8,128)S(1)} %copy-done, f32[1,1,64,512]{3,2,1,0:T(8,128)S(1)} %copy-done.2, f32[1,1,64,512]{3,2,1,0:T(8,128)S(1)} %copy-done.3, f32[1,64,512]{2,1,0:T(8,128)S(1)} %copy-done.4, s32[1,1,32,2048]{3,2,1,0:T(8,128)S(1)} %copy-done.1, ...), custom_call_target="tpu_custom_call" | custom-call | tf_op jit(solution)/shard_map/pallas_call | solution.py:236
  47.5 0.7 %copy.12 = f32[1,1,64,512]{3,2,1,0:T(8,128)} copy(f32[1,1,64,512]{3,2,1,0:T(8,128)S(1)} %get-tuple-element.4) | data formatting | bytes 262144
  48.2 0.8 %copy.13 = bf16[1,1,512,512]{3,2,1,0:T(8,128)(2,1)} copy(bf16[1,1,512,512]{3,2,1,0:T(8,128)(2,1)S(1)} %get-tuple-element.5) | data formatting | bytes 1048576
Async XLA Ops:
  0.6 0.8 %copy-start.5 = (f32[1,512]{1,0:T(1,128)S(1)}, f32[1,512]{1,0:T(1,128)}, u32[]{:S(2)}) copy-start(f32[1,512]{1,0:T(1,128)} %gain_hbm.1) | copy-start | bytes 6148
  1.4 1.2 %copy-start = (f32[1,1,512,512]{3,2,1,0:T(8,128)S(1)}, f32[1,1,512,512]{3,2,1,0:T(8,128)}, u32[]{:S(2)}) copy-start(f32[1,1,512,512]{3,2,1,0:T(8,128)} %t_hbm.1) | copy-start | bytes 3145732
  2.7 0.9 %copy-start.1 = (s32[1,1,32,2048]{3,2,1,0:T(8,128)S(1)}, s32[1,1,32,2048]{3,2,1,0:T(8,128)}, u32[]{:S(2)}) copy-start(s32[1,1,32,2048]{3,2,1,0:T(8,128)} %inc_hbm.1) | copy-start | bytes 786436
  3.6 0.9 %copy-start.2 = (f32[1,1,64,512]{3,2,1,0:T(8,128)S(1)}, f32[1,1,64,512]{3,2,1,0:T(8,128)}, u32[]{:S(2)}) copy-start(f32[1,1,64,512]{3,2,1,0:T(8,128)} %s_hbm.1) | copy-start | bytes 393220
  4.5 0.9 %copy-start.3 = (f32[1,1,64,512]{3,2,1,0:T(8,128)S(1)}, f32[1,1,64,512]{3,2,1,0:T(8,128)}, u32[]{:S(2)}) copy-start(f32[1,1,64,512]{3,2,1,0:T(8,128)} %cot_hbm.1) | copy-start | bytes 393220
  5.4 0.9 %copy-start.4 = (f32[1,64,512]{2,1,0:T(8,128)S(1)}, f32[1,64,512]{2,1,0:T(8,128)}, u32[]{:S(2)}) copy-start(f32[1,64,512]{2,1,0:T(8,128)} %term_hbm.1) | copy-start | bytes 393220

commit v2 on v1

v2 whole, which is shorter than its diff:
```python
import functools

import jax
import jax.numpy as jnp
from jax import lax
from jax.experimental import pallas as pl
from jax.experimental.pallas import tpu as pltpu
from jax.sharding import PartitionSpec as P

CHUNKS = 4
F32 = jnp.float32
BF16 = jnp.bfloat16
MESH = pl.DeviceIdType.MESH


def split(value):
    high = value.astype(BF16)
    return high, (value - high.astype(F32)).astype(BF16)


def dot(left, right, dims=((1,), (0,))):
    return lax.dot_general(left, right, (dims, ((), ())), preferred_element_type=F32)


def kernel(
    teams, steps, chunks, slabs,
    t_hbm, s_hbm, cot_hbm, term_hbm, inc_hbm, meas_hbm, gain_hbm,
    out, grad,
    t_vm, s_vm, gain_vm, th, tl, s3, x3, xin, adj,
    meas, inc, part, parts,
    local_sem, inc_send, inc_recv, meas_send, meas_recv, part_send, part_recv,
    fwd_send, x_send, x_recv, cot_sem, t_send, t_recv,
):
    me = lax.axis_index("team")
    step = lax.axis_index("tm")
    odd = lax.rem(step, 2)
    even = 1 - odd
    partner = step + 1 - 2 * odd
    side = lax.rem(me, 2)
    paired = step < steps - 2
    leader = paired & (side == odd)
    helper = paired & (side == even)
    ended = step == steps - 1
    hands_on = leader | jnp.logical_not(paired)
    skips = (step >= 2) & (leader | ((step == steps - 2) & (side == 0)))
    forwards = (step > 0) & hands_on
    slot = lax.max(odd, leader.astype(jnp.int32))
    cols, width = xin.shape
    robots, cut = inc.shape[1:]
    rows = cols // chunks
    peers = [lax.rem(me + d, teams) for d in range(teams)]
    behind = [lax.rem(me + teams - d, teams) for d in range(teams)]

    barrier = pltpu.get_barrier_semaphore()

    def greet(team, at):
        pl.semaphore_signal(barrier, inc=1, device_id={"team": team, "tm": at}, device_id_type=MESH)

    for d in range(teams):
        if d:
            greet(peers[d], step)
        greet(peers[d], partner)
    met = 2 * teams - 1
    beside = step - 1 + 2 * odd
    for at in (beside, step - 2, step + 2):
        inside = (at >= 0) & (at < steps)

        @pl.when(inside)
        def _():
            greet(me, at)

        met = met + inside.astype(jnp.int32)

    def columns(owner):
        return inc_hbm.at[0, 0, :, pl.ds(pl.multiple_of(owner * cut, cut), cut)]

    loads = [
        pltpu.make_async_copy(t_hbm.at[0, 0], t_vm.at[odd], local_sem.at[0]),
        pltpu.make_async_copy(cot_hbm.at[0, 0], adj.at[odd], local_sem.at[1]),
        pltpu.make_async_copy(s_hbm.at[0, 0], s_vm, local_sem.at[2]),
        pltpu.make_async_copy(meas_hbm.at[0, 0], meas.at[0], local_sem.at[3]),
        pltpu.make_async_copy(gain_hbm, gain_vm, local_sem.at[4]),
        pltpu.make_async_copy(columns(me), inc.at[0], local_sem.at[5]),
    ]
    for load in loads:
        load.start()
    terminal = pltpu.make_async_copy(term_hbm.at[0], xin, local_sem.at[6])

    @pl.when(ended)
    def _():
        terminal.start()

    def remote(src, dst, send, recv, team, at):
        return pltpu.make_async_remote_copy(
            src_ref=src, dst_ref=dst, send_sem=send, recv_sem=recv,
            device_id={"team": team, "tm": at}, device_id_type=MESH)

    inc_copies = [
        remote(columns(peers[d]), inc.at[d], inc_send.at[d], inc_recv.at[d], peers[d], step)
        for d in range(1, teams)
    ]
    meas_copies = [
        remote(meas_hbm.at[0, 0], meas.at[d], meas_send.at[d], meas_recv.at[d], peers[d], step)
        for d in range(1, teams)
    ]
    slab = width // slabs
    t_copies = [
        remote(t_hbm.at[0, 0, pl.ds(i * slab, slab)], t_vm.at[odd, pl.ds(i * slab, slab)],
               t_send.at[i], t_recv.at[i], me, partner)
        for i in range(slabs)
    ]
    t_arrivals = [
        remote(t_hbm.at[0, 0, pl.ds(i * slab, slab)], t_vm.at[even, pl.ds(i * slab, slab)],
               t_send.at[i], t_recv.at[i], me, partner)
        for i in range(slabs)
    ]
    cot_copy = remote(cot_hbm.at[0, 0], adj.at[odd], cot_sem.at[0], cot_sem.at[1], me, partner)
    cot_arrival = remote(cot_hbm.at[0, 0], adj.at[even], cot_sem.at[0], cot_sem.at[1], me, partner)

    pl.semaphore_wait(barrier, met)
    for copy in meas_copies + inc_copies:
        copy.start()

    @pl.when(helper)
    def _():
        cot_copy.start()
        for copy in t_copies:
            copy.start()

    def divide(which, start, stop):
        @pl.loop(start // 64, stop // 64)
        def _(i):
            band = pl.ds(pl.multiple_of(i * 64, 64), 64)
            high, low = split(t_vm[which, band, :])
            th[which, band, :] = high
            tl[which, band, :] = low

    loads[0].wait()
    divide(odd, 0, width)
    loads[1].wait()
    loads[2].wait()
    high, low = split(s_vm[...])
    s3[0:cols, :] = high
    s3[cols:2 * cols, :] = high
    s3[2 * cols:3 * cols, :] = low

    def times_transition(which, high, low):
        both = jnp.concatenate([high, low], axis=0)
        wide = dot(both, th[which])
        n = high.shape[0]
        return wide[:n] + wide[n:] + dot(high, tl[which])

    def keep(at, n, high, low):
        x3[at:at + n, :] = high
        x3[cols + at:cols + at + n, :] = low
        x3[2 * cols + at:2 * cols + at + n, :] = high

    loads[3].wait()
    loads[4].wait()
    loads[5].wait()
    landmark = jnp.zeros((2 * cols, cut), F32)
    seen = []
    for d in range(teams):
        if d:
            meas_copies[d - 1].wait_recv()
            inc_copies[d - 1].wait_recv()
        seen.append(inc[d].astype(F32).astype(BF16))
        high, low = split(meas[d])
        landmark = landmark + dot(jnp.concatenate([high, low], axis=1), seen[d], ((0,), (0,)))
    high, low = split(landmark[:cols] + landmark[cols:])
    both = jnp.concatenate([high, low], axis=0)

    def part_copy(d, parity, which, at):
        return remote(
            part.at[d], parts.at[parity, d], part_send.at[which, d], part_recv.at[parity, d], behind[d], at)

    for d in range(teams):
        piece = dot(both, seen[d], ((1,), (1,)))
        piece = piece[:cols] + piece[cols:]
        part[d] = piece
        if d:
            part_copy(d, odd, 0, step).start()
        else:
            parts[odd, 0] = piece

        @pl.when(paired & (lax.rem(behind[d], 2) == even))
        def _():
            part_copy(d, odd, 1, partner).start()

    @pl.when(ended)
    def _():
        terminal.wait()
        high, low = split(xin[...])
        adj[1] += times_transition(1, high, low)

        keep(0, cols, high, low)

    states = width // robots
    robot = lax.broadcasted_iota(jnp.int32, (robots, width), 0)
    state = lax.broadcasted_iota(jnp.int32, (robots, width), 1)
    lower = robot * states
    pick = jnp.where((state >= lower) & (state < lower + states), 1.0, 0.0).astype(BF16)

    def inject(parity, first):
        for d in range(first, teams):
            part_copy(d, parity, 0, step).wait_recv()
        injection = parts[parity, 0]
        for d in range(1, teams):
            injection = injection + parts[parity, d]
        high, low = split(injection)
        spread = dot(jnp.concatenate([high, low], axis=0), pick)
        adj[parity] += (spread[:cols] + spread[cols:]) * gain_vm[...]

    inject(odd, 1)

    @pl.when(leader)
    def _():
        cot_arrival.wait_recv()
        inject(even, 0)
        for i in range(slabs):
            t_arrivals[i].wait_recv()
            divide(even, i * slab, (i + 1) * slab)

    def band(i):
        return pl.ds(i * rows, rows)

    x_copies = [
        remote(adj.at[0, band(i)], xin.at[band(i)], x_send.at[i], x_recv.at[i], me, lax.max(step - 2, 0))
        for i in range(chunks)
    ]
    fwd_copies = [
        remote(adj.at[odd, band(i)], xin.at[band(i)], fwd_send.at[i], x_recv.at[i], me, lax.max(step - 1, 0))
        for i in range(chunks)
    ]
    for i in range(chunks):
        at = i * rows

        @pl.when(jnp.logical_not(ended))
        def _():
            x_copies[i].wait_recv()
            high, low = split(xin[at:at + rows, :])
            adj[slot, at:at + rows, :] += times_transition(slot, high, low)

            @pl.when(slot == odd)
            def _():
                keep(at, rows, high, low)

        @pl.when(forwards & (odd == 1))
        def _():
            fwd_copies[i].start()

        @pl.when(leader)
        def _():
            high, low = split(adj[1, at:at + rows, :])
            adj[0, at:at + rows, :] += times_transition(0, high, low)

            @pl.when(odd == 0)
            def _():
                keep(at, rows, high, low)

        @pl.when(skips)
        def _():
            x_copies[i].start()

        @pl.when(forwards & (odd == 0))
        def _():
            fwd_copies[i].start()

    blocks = 4
    high = width // blocks
    for b in range(blocks):
        at = slice(b * high, (b + 1) * high)
        grad[0, 0, at, :] = dot(x3[:, at], s3[...], ((0,), (0,))).astype(BF16)
    out[0, 0] = adj[odd]

    for copy in meas_copies + inc_copies:
        copy.wait_send()
    for d in range(teams):
        if d:
            part_copy(d, odd, 0, step).wait_send()

        @pl.when(paired & (lax.rem(behind[d], 2) == even))
        def _():
            part_copy(d, odd, 1, partner).wait_send()

    @pl.when(helper)
    def _():
        for copy in t_copies:
            copy.wait_send()
        cot_copy.wait_send()

    @pl.when(skips)
    def _():
        for copy in x_copies:
            copy.wait_send()

    @pl.when(forwards)
    def _():
        for copy in fwd_copies:
            copy.wait_send()


def shards(teams, steps, transitions, states, cotangent, terminal, incidence, measured, obs_gain):
    cols, width = terminal.shape[1:]
    robots, landmarks = incidence.shape[2:]
    cut = landmarks // teams
    chunks = CHUNKS
    slabs = 1
    dma = pltpu.SemaphoreType.DMA
    remote = pl.BlockSpec(memory_space=pltpu.HBM)
    local = pl.BlockSpec(memory_space=pltpu.VMEM)
    return pl.pallas_call(
        functools.partial(kernel, teams, steps, chunks, slabs),
        out_shape=(
            jax.ShapeDtypeStruct((1, 1, cols, width), F32),
            jax.ShapeDtypeStruct((1, 1, width, width), BF16),
        ),
        in_specs=[remote] * 7,
        out_specs=(local, local),
        scratch_shapes=[
            pltpu.VMEM((2, width, width), F32),
            pltpu.VMEM((cols, width), F32),
            pltpu.VMEM((1, width), F32),
            pltpu.VMEM((2, width, width), BF16),
            pltpu.VMEM((2, width, width), BF16),
            pltpu.VMEM((3 * cols, width), BF16),
            pltpu.VMEM((3 * cols, width), BF16),
            pltpu.VMEM((cols, width), F32),
            pltpu.VMEM((2, cols, width), F32),
            pltpu.VMEM((teams, robots, cols), F32),
            pltpu.VMEM((teams, robots, cut), jnp.int32),
            pltpu.VMEM((teams, cols, robots), F32),
            pltpu.VMEM((2, teams, cols, robots), F32),
            dma((7,)),
            dma((teams,)), dma((teams,)), dma((teams,)), dma((teams,)),
            dma((2, teams)), dma((2, teams)),
            dma((chunks,)), dma((chunks,)), dma((chunks,)),
            dma((2,)), dma((slabs,)), dma((slabs,)),
        ],
        compiler_params=pltpu.CompilerParams(
            collective_id=0, has_side_effects=True, vmem_limit_bytes=63 * 1024 * 1024),
    )(transitions, states, cotangent, terminal, incidence, jnp.swapaxes(measured, 2, 3), obs_gain)


def solution(mesh):
    placed = (
        P("team", "tm", None, None),
        P("team", "tm", None, None),
        P("team", "tm", None, None),
        P("team", None, None),
        P("team", "tm", None, None),
        P("team", "tm", None, None),
        P("team", None),
    )
    return jax.shard_map(
        functools.partial(shards, mesh.shape["team"], mesh.shape["tm"]),
        mesh=mesh,
        in_specs=placed,
        out_specs=(P("team", "tm", None, None), P("team", "tm", None, None)),
        check_vma=False,
    )
```

time: 49.2 us -> 39.8 us (0.81)
  the two profiles are of different devices: /device:TPU:0 before, /device:TPU:1 now
where the time goes in v2:
time: 39.8 us; the launch traced here: 39.6 us
  Pallas kernels  35.5 us (89%)
  local copies, waits for them, and re-layouts  3.44 us (9%)
  between operations  0.64 us (2%)
    pallas_call x1, Pallas kernels, shards(): pl.pallas_call(functools.partial(kernel, teams, steps, chunks, slabs), ou...  35.5 us
    unnamed x2, local copies, waits for them, and re-layouts  3.44 us

profile of v2, /device:TPU:1, one launch (start us, length us, event | category | flops | bytes accessed | tf_op | source)
XLA Modules:
  0.0 39.6 jit_solution(12470607879315678610)
XLA Ops:
  0.6 35.5 %shard_map.86 = (f32[1,1,64,512]{3,2,1,0:T(8,128)}, bf16[1,1,512,512]{3,2,1,0:T(8,128)(2,1)}) custom-call(f32[1,1,512,512]{3,2,1,0:T(8,128)} %t_hbm.1, f32[1,1,64,512]{3,2,1,0:T(8,128)} %s_hbm.1, f32[1,1,64,512]{3,2,1,0:T(8,128)} %cot_hbm.1, f32[1,64,512]{2,1,0:T(8,128)} %term_hbm.1, s32[1,1,32,2048]{3,2,1,0:T(8,128)} %inc_hbm.1, f32[1,1,32,64]{3,2,1,0:T(8,128)} %bitcast.1, ...), custom_call_target="tpu_custom_call" | custom-call | tf_op jit(solution)/shard_map/pallas_call | solution.py:312
  36.1 1.6 %copy.11 = f32[1,1,64,512]{3,2,1,0:T(8,128)} copy(f32[1,1,64,512]{3,2,1,0:T(8,128)} %get-tuple-element.4) | data formatting | bytes 262144
  37.7 1.9 %copy.12 = bf16[1,1,512,512]{3,2,1,0:T(8,128)(2,1)} copy(bf16[1,1,512,512]{3,2,1,0:T(8,128)(2,1)} %get-tuple-element.5) | data formatting | bytes 1048576

commit v3 on v2

--- a/solution.py
+++ b/solution.py
@@ -25,8 +25,8 @@
 def kernel(
     teams, steps, chunks, slabs,
     t_hbm, s_hbm, cot_hbm, term_hbm, inc_hbm, meas_hbm, gain_hbm,
-    out, grad,
-    t_vm, s_vm, gain_vm, th, tl, s3, x3, xin, adj,
+    out, x3, s3,
+    t_vm, s_vm, gain_vm, th, tl, xin, adj,
     meas, inc, part, parts,
     local_sem, inc_send, inc_recv, meas_send, meas_recv, part_send, part_recv,
     fwd_send, x_send, x_recv, cot_sem, t_send, t_recv,
@@ -37,12 +37,12 @@
     even = 1 - odd
     partner = step + 1 - 2 * odd
     side = lax.rem(me, 2)
-    paired = step < steps - 2
+    paired = step < steps - 4
     leader = paired & (side == odd)
     helper = paired & (side == even)
     ended = step == steps - 1
     hands_on = leader | jnp.logical_not(paired)
-    skips = (step >= 2) & (leader | ((step == steps - 2) & (side == 0)))
+    skips = (step >= 2) & (leader | ((step == steps - 4) & (side == 0)))
     forwards = (step > 0) & hands_on
     slot = lax.max(odd, leader.astype(jnp.int32))
     cols, width = xin.shape
@@ -266,11 +266,6 @@
         def _():
             fwd_copies[i].start()
 
-    blocks = 4
-    high = width // blocks
-    for b in range(blocks):
-        at = slice(b * high, (b + 1) * high)
-        grad[0, 0, at, :] = dot(x3[:, at], s3[...], ((0,), (0,))).astype(BF16)
     out[0, 0] = adj[odd]
 
     for copy in meas_copies + inc_copies:
@@ -309,22 +304,21 @@
     dma = pltpu.SemaphoreType.DMA
     remote = pl.BlockSpec(memory_space=pltpu.HBM)
     local = pl.BlockSpec(memory_space=pltpu.VMEM)
-    return pl.pallas_call(
+    adjoint, x3, s3 = pl.pallas_call(
         functools.partial(kernel, teams, steps, chunks, slabs),
         out_shape=(
             jax.ShapeDtypeStruct((1, 1, cols, width), F32),
-            jax.ShapeDtypeStruct((1, 1, width, width), BF16),
+            jax.ShapeDtypeStruct((3 * cols, width), BF16),
+            jax.ShapeDtypeStruct((3 * cols, width), BF16),
         ),
         in_specs=[remote] * 7,
-        out_specs=(local, local),
+        out_specs=(local, local, local),
         scratch_shapes=[
             pltpu.VMEM((2, width, width), F32),
             pltpu.VMEM((cols, width), F32),
             pltpu.VMEM((1, width), F32),
             pltpu.VMEM((2, width, width), BF16),
             pltpu.VMEM((2, width, width), BF16),
-            pltpu.VMEM((3 * cols, width), BF16),
-            pltpu.VMEM((3 * cols, width), BF16),
             pltpu.VMEM((cols, width), F32),
             pltpu.VMEM((2, cols, width), F32),
             pltpu.VMEM((teams, robots, cols), F32),
@@ -340,6 +334,8 @@
         compiler_params=pltpu.CompilerParams(
             collective_id=0, has_side_effects=True, vmem_limit_bytes=63 * 1024 * 1024),
     )(transitions, states, cotangent, terminal, incidence, jnp.swapaxes(measured, 2, 3), obs_gain)
+    grad = dot(x3, s3, ((0,), (0,))).astype(BF16)
+    return adjoint, grad[None, None]
 
 
 def solution(mesh):

time: 39.8 us -> 38.8 us (0.975)
  the two profiles are of different devices: /device:TPU:1 before, /device:TPU:0 now
where the time goes in v3:
time: 38.8 us; the launch traced here: 38.7 us
  Pallas kernels  35.2 us (91%)
  matrix products  2.19 us (6%)
  local copies, waits for them, and re-layouts  0.66 us (2%)
  between operations  0.65 us (2%)
    pallas_call x1, Pallas kernels, shards(): pl.pallas_call(functools.partial(kernel, teams, steps, chunks, slabs), ou...  35.2 us
    dot_general x1, matrix products, dot(): lax.dot_general(left, right, (dims, ((), ())), preferred_element_type=F32)  2.19 us

profile of v3, /device:TPU:0, one launch (start us, length us, event | category | flops | bytes accessed | tf_op | source)
XLA Modules:
  0.0 38.7 jit_solution(5011534757899141558)
XLA Ops:
  0.6 35.2 %shard_map.86 = (f32[1,1,64,512]{3,2,1,0:T(8,128)}, bf16[192,512]{1,0:T(8,128)(2,1)}, bf16[192,512]{1,0:T(8,128)(2,1)}) custom-call(f32[1,1,512,512]{3,2,1,0:T(8,128)} %t_hbm.1, f32[1,1,64,512]{3,2,1,0:T(8,128)} %s_hbm.1, f32[1,1,64,512]{3,2,1,0:T(8,128)} %cot_hbm.1, f32[1,64,512]{2,1,0:T(8,128)} %term_hbm.1, s32[1,1,32,2048]{3,2,1,0:T(8,128)} %inc_hbm.1, ...), custom_call_target="tpu_custom_call" | custom-call | tf_op jit(solution)/shard_map/pallas_call | solution.py:307
  35.8 0.0 copy-start
  35.8 2.2 %fusion = bf16[1,1,512,512]{3,2,1,0:T(8,128)(2,1)} fusion(bf16[192,512]{1,0:T(8,128)(2,1)} %get-tuple-element.6, bf16[192,512]{1,0:T(8,128)(2,1)} %get-tuple-element.7), kind=kOutput, calls=%fused_computation.1 | convolution fusion | flops 100925440 | bytes 917504 | tf_op jit(solution)/shard_map/dot_general | solution.py:22
  38.0 0.0 copy-done
  38.0 0.7 %copy.10 = f32[1,1,64,512]{3,2,1,0:T(8,128)} copy(f32[1,1,64,512]{3,2,1,0:T(8,128)S(1)} %copy-done) | data formatting | bytes 262144
Async XLA Ops:
  35.8 2.2 %copy-start = (f32[1,1,64,512]{3,2,1,0:T(8,128)S(1)}, f32[1,1,64,512]{3,2,1,0:T(8,128)}, u32[]{:S(2)}) copy-start(f32[1,1,64,512]{3,2,1,0:T(8,128)} %get-tuple-element.10) | copy-start | bytes 393220
